TPU v7x, 32 devices: a whole 2x2x4 slice. The times are simulated.
32 devices in a mesh: pair: 8 (over z, y), aux: 4 (over x, core).
Axes of the slice: x: 2, y: 2, z: 4, core: 2. Of those that a mesh axis runs over, the one named last changes fastest.
Arguments:
- amplitudes: bfloat16 [128, 16384], P('pair'), may hold values from -0.059814453 to 0.059814453
- factor_ca: bfloat16 [6400, 16384], P(('pair', 'aux')), may hold values from -0.5 to 0.5
- factor_db: bfloat16 [6400, 16384], P(('pair', 'aux')), may hold values from -0.5 to 0.5
Outputs:
- ladder: bfloat16 [128, 16384], P('pair', 'aux')
All inputs are finite; a program needn't handle non-finite values.
Results may differ from a plain program's by a relative error of at most 0.02.
Values may be sent and summed in bfloat16 or wider, within the bound.
A program may use at most 192 MiB of HBM per device.

v0:
```python
import functools

import jax
import jax.numpy as jnp
from jax import lax
from jax.experimental import pallas as pl
from jax.experimental.pallas import tpu as pltpu
from jax.sharding import PartitionSpec as P

A = 128
B = 128
C = 128
D = 128
NA = 8
DC = 8


def ladder_kernel(x_ref, y_ref, t_ref, o_ref, xt, s, acc):
    xt[...] = x_ref[...].T
    acc[...] = jnp.zeros_like(acc)

    @pl.loop(0, D // DC)
    def _(j):
        for dd in range(0, DC, 2):
            cols = pl.ds(pl.multiple_of((j * DC + dd) * B, 2 * B), 2 * B)
            v = jnp.dot(xt[...], y_ref[:, cols], preferred_element_type=jnp.float32)
            v = v.astype(jnp.bfloat16)
            for a in range(NA):
                for e in range(2):
                    s[(dd + e) * C:(dd + e + 1) * C, a * B:(a + 1) * B] = v[
                        a * C:(a + 1) * C, e * B:(e + 1) * B
                    ]
        tc = pl.ds(pl.multiple_of(j * DC * C, DC * C), DC * C)
        acc[...] += jnp.dot(t_ref[:, tc], s[...], preferred_element_type=jnp.float32)

    o_ref[...] = acc[...].astype(jnp.bfloat16)


def partial_ladder(x, y, t):
    rows, a_cols = x.shape
    n_ij = t.shape[0]
    na = a_cols // C
    return pl.pallas_call(
        ladder_kernel,
        grid=(na // NA,),
        in_specs=[
            pl.BlockSpec((rows, NA * C), lambda i: (0, i)),
            pl.BlockSpec((rows, D * B), lambda i: (0, 0), pipeline_mode=pl.Buffered(1)),
            pl.BlockSpec((n_ij, D * C), lambda i: (0, 0), pipeline_mode=pl.Buffered(1)),
        ],
        out_specs=pl.BlockSpec((n_ij, NA * B), lambda i: (0, i)),
        out_shape=jax.ShapeDtypeStruct((n_ij, na * B), jnp.bfloat16),
        scratch_shapes=[
            pltpu.VMEM((NA * C, rows), jnp.bfloat16),
            pltpu.VMEM((DC * C, NA * B), jnp.bfloat16),
            pltpu.VMEM((n_ij, NA * B), jnp.float32),
        ],
        compiler_params=pltpu.CompilerParams(vmem_limit_bytes=56 << 20),
        cost_estimate=pl.CostEstimate(
            flops=2 * na * C * D * B * (rows + n_ij),
            bytes_accessed=2 * rows * (a_cols + D * B),
            transcendentals=0,
        ),
    )(x, y, t)


def local(amplitudes, factor_ca, factor_db):
    n_aux = lax.axis_size("aux")
    n_x = n_aux // 2
    aux = lax.axis_index("aux")
    core = lax.rem(aux, 2)
    chip = aux // 2
    rows = factor_ca.shape[0]
    n_pair_rows = amplitudes.shape[0]
    a_share = A // n_aux
    swap = [(i, i ^ 1) for i in range(n_aux)]

    t_own = amplitudes.reshape(n_pair_rows, C, D).transpose(0, 2, 1).reshape(n_pair_rows, D * C)
    t = lax.all_gather(t_own, "pair", axis=0, tiled=True)

    x_t = factor_ca.reshape(rows, C, A).transpose(0, 2, 1)
    x_t = x_t.reshape(rows, n_x, 2, a_share * C)
    x_mine = lax.dynamic_index_in_dim(x_t, core, 2, keepdims=False).reshape(rows, -1)
    x_give = lax.dynamic_index_in_dim(x_t, 1 - core, 2, keepdims=False).reshape(rows, -1)
    y_other = lax.ppermute(factor_db, "aux", swap)
    x_other = lax.ppermute(x_give, "aux", swap)
    x = jnp.concatenate([x_mine, x_other], axis=0)
    y = jnp.concatenate([factor_db, y_other], axis=0)

    part = partial_ladder(x, y, t)
    n_ij = part.shape[0]
    part = part.reshape(n_ij, n_x, a_share * B)
    total = lax.dynamic_index_in_dim(part, chip, 1, keepdims=False).astype(jnp.float32)
    for k in range(1, n_x):
        give = lax.dynamic_index_in_dim(part, lax.rem(chip + k, n_x), 1, keepdims=False)
        hop = [(i, (i + 2 * k) % n_aux) for i in range(n_aux)]
        total = total + lax.ppermute(give, "aux", hop).astype(jnp.float32)
    return lax.psum_scatter(
        total.astype(jnp.bfloat16), "pair", scatter_dimension=0, tiled=True
    )


def solution(mesh):
    return jax.shard_map(
        local,
        mesh=mesh,
        in_specs=(P("pair", None), P(("pair", "aux"), None), P(("pair", "aux"), None)),
        out_specs=P("pair", "aux"),
        check_vma=False,
    )
```

profile of v0, /device:TPU:0, one launch (start us, length us, event | category | flops | bytes accessed | tf_op | source)
XLA Modules:
  0.0 496.7 jit_solution(12035616587855091349)
XLA Ops:
  6.5 0.5 collective-permute-start.1
  7.0 1.1 copy.19
  8.1 0.3 copy.11
  8.4 1.1 copy.27
  9.5 0.0 all-gather.2.cloned.1.call-update
  9.6 0.0 reduce-scatter.2.cloned.1.call-start
  9.6 7.6 %copy.16 = bf16[25,8,128,128]{3,2,1,0:T(8,128)(2,1)} copy(bf16[25,8,128,128]{3,1,2,0:T(8,128)(2,1)} %bitcast.27) | data formatting | bytes 13107200
  17.2 9.6 %copy.10 = bf16[200,128,128]{1,2,0:T(8,128)(2,1)} copy(bf16[200,128,128]{2,1,0:T(8,128)(2,1)} %bitcast.23) | data formatting | bytes 13107200 | tf_op jit(solution)/shard_map/reshape | solution.py:81
  26.8 13.4 %reshape.26 = bf16[200,2,2,4096]{3,2,1,0:T(2,128)(2,1)} reshape(bf16[200,128,128]{2,1,0:T(8,128)(2,1)} %bitcast.22) | data formatting | bytes 13107200 | tf_op jit(solution)/shard_map/reshape | solution.py:82
  40.3 53.1 %dynamic-slice_reduce_fusion = bf16[200,2,4096]{2,1,0:T(2,128)(2,1)S(1)} fusion(bf16[200,2,2,4096]{3,2,1,0:T(2,128)(2,1)} %reshape.26, s32[]{:T(128)S(6)} %select_n.20), kind=kLoop, calls=%fused_computation.2 | loop fusion | bytes 6553604 | tf_op jit(solution)/shard_map/jit(dynamic_index_in_dim)/dynamic_slice | solution.py:84
  93.4 3.9 copy.18
  97.3 53.1 %dynamic-slice_reduce_fusion.1 = bf16[200,2,4096]{2,1,0:T(2,128)(2,1)S(1)} fusion(bf16[200,2,2,4096]{3,2,1,0:T(2,128)(2,1)} %reshape.26, s32[]{:T(128)S(6)} %select_n.19), kind=kLoop, calls=%fused_computation.3 | loop fusion | bytes 6553604 | tf_op jit(solution)/shard_map/jit(dynamic_index_in_dim)/dynamic_slice | solution.py:83
  150.4 2.2 copy.17
  152.7 5.3 %pad_maximum_fusion.1.x_ref = bf16[400,8192]{1,0:T(8,128)(2,1)} fusion(bf16[200,8192]{1,0:T(8,128)(2,1)} %collective-permute-done, bf16[200,8192]{1,0:T(8,128)(2,1)S(1)} %bitcast.24), kind=kLoop, calls=%fused_computation.1 | loop fusion | flops 13107200 | bytes 13107200 | tf_op jit(solution)/shard_map/concatenate | solution.py:87
  158.0 12.2 %pad_maximum_fusion.y_ref = bf16[400,16384]{1,0:T(8,128)(2,1)} fusion(bf16[200,16384]{1,0:T(8,128)(2,1)} %collective-permute-done.1, bf16[200,16384]{1,0:T(8,128)(2,1)} %param.5), kind=kLoop, calls=%fused_computation | loop fusion | flops 26214400 | bytes 26214400 | tf_op jit(solution)/shard_map/concatenate | solution.py:88
  170.2 215.8 %shard_map.37 = bf16[128,8192]{1,0:T(8,128)(2,1)} custom-call(bf16[400,8192]{1,0:T(8,128)(2,1)} %pad_maximum_fusion.1.x_ref, bf16[400,16384]{1,0:T(8,128)(2,1)} %pad_maximum_fusion.y_ref, bf16[128,16384]{1,0:T(8,128)(2,1)} %all-gather.2.cloned.1.call-done.t_ref), custom_call_target="tpu_custom_call" | custom-call | flops 141733920768 | bytes 19660800 | tf_op jit(solution)/shard_map/pallas_call | solution.py:43
  386.0 3.6 reshape.31
  389.6 4.9 constant_dynamic-slice_fusion.1
  394.4 1.1 copy.26
  395.6 2.9 collective-permute-start.2
  398.5 23.5 %collective-permute-done.2 = bf16[128,4096]{1,0:T(8,128)(2,1)S(1)} collective-permute-done((bf16[128,4096]{1,0:T(8,128)(2,1)S(1)}, bf16[128,4096]{1,0:T(8,128)(2,1)S(1)}, u32[]{:S(2)}, u32[]{:S(2)}) %collective-permute-start.2) | collective-permute-done | bytes 1048608 | tf_op jit(solution)/shard_map/ppermute | solution.py:97
  421.9 2.2 fusion
  424.2 0.0 reduce-scatter.2.cloned.1.call-update
  424.2 65.7 %reduce-scatter.2.cloned.1.call-done = bf16[16,4096]{1,0:T(8,128)(2,1)} async-done(((bf16[128,4096]{1,0:T(8,128)(2,1)}), bf16[16,4096]{1,0:T(8,128)(2,1)}) %reduce-scatter.2.cloned.1.call-update) | async-done | bytes 131088 | tf_op jit(solution)/shard_map/reduce_scatter | solution.py:98
  (5 shorter events, 0.0 us)
Async XLA Ops:
  6.5 163.6 %all-gather.2.cloned.1.call-start = ((), (), s32[]{:S(2)}) async-start(), calls=%async_computation.1 | async-start | bytes 4718592 | tf_op jit(solution)/shard_map/all_gather | solution.py:79
  6.5 151.4 %collective-permute-start.1 = (bf16[200,16384]{1,0:T(8,128)(2,1)}, bf16[200,16384]{1,0:T(8,128)(2,1)}, u32[]{:S(2)}, u32[]{:S(2)}) collective-permute-start(bf16[200,16384]{1,0:T(8,128)(2,1)} %param.5), channel_id=1, source_target_pairs={{0,1},{1,0},{2,3},{3,2},{4,5},{5,4},{6,7},{7,6},{8,9},{9,8},{10,11... | collective-permute-start | bytes 19660808 | tf_op jit(solution)/shard_map/ppermute | solution.py:85
  9.6 480.3 %reduce-scatter.2.cloned.1.call-start = ((), (), s32[]{:S(2)}) async-start(), calls=%async_computation.2 | async-start | bytes 1179648 | tf_op jit(solution)/shard_map/reduce_scatter | solution.py:98
  97.3 55.4 %collective-permute-start = (bf16[200,8192]{1,0:T(8,128)(2,1)}, bf16[200,8192]{1,0:T(8,128)(2,1)}, u32[]{:S(2)}, u32[]{:S(2)}) collective-permute-start(bf16[200,8192]{1,0:T(8,128)(2,1)} %bitcast.10), channel_id=1, source_target_pairs={{0,1},{1,0},{2,3},{3,2},{4,5},{5,4},{6,7},{7,6},{8,9},{9,8},{10,11... | collective-permute-start | bytes 9830408 | tf_op jit(solution)/shard_map/ppermute | solution.py:86
  395.6 26.4 %collective-permute-start.2 = (bf16[128,4096]{1,0:T(8,128)(2,1)S(1)}, bf16[128,4096]{1,0:T(8,128)(2,1)S(1)}, u32[]{:S(2)}, u32[]{:S(2)}) collective-permute-start(bf16[128,4096]{1,0:T(8,128)(2,1)S(1)} %bitcast.31), channel_id=1, source_target_pairs={{0,2},{1,3},{2,0},{3,1},{4,6},{5,7},{6,4},{7,5},{8,10},{9,11},{10,... | collective-permute-start | bytes 3145736 | tf_op jit(solution)/shard_map/ppermute | solution.py:97
Sparse Core Ops, SparseCore 0:
  9.7 75.8 all-gather.1
  424.3 65.4 reduce-scatter.1
where the time goes:
time: 498 us; the launch traced here: 497 us
  Pallas kernels  216 us (43%)
  local copies, waits for them, and re-layouts  155 us (31%)
  waiting for transfers between devices  89.2 us (18%)
  other arithmetic  19.8 us (4%)
  between operations  13.5 us (3%)
    pallas_call x1, Pallas kernels, partial_ladder(): pl.pallas_call(ladder_kernel, grid=(na // NA,), in_specs=[pl.BlockSpec((r...  216 us
    reduce_scatter x1, waiting for transfers between devices, local(): lax.psum_scatter(total.astype(jnp.bfloat16), 'pair', scatter_dimension=0,...  65.7 us
    dynamic_slice x1, local copies, waits for them, and re-layouts, local(): lax.dynamic_index_in_dim(x_t, core, 2, keepdims=False).reshape(rows, -1)  53.1 us
    dynamic_slice x1, local copies, waits for them, and re-layouts, local(): lax.dynamic_index_in_dim(x_t, 1 - core, 2, keepdims=False).reshape(rows, -1)  53.1 us
    ppermute x1, waiting for transfers between devices, local(): total = total + lax.ppermute(give, 'aux', hop).astype(jnp.float32)  23.5 us
    unnamed x6, local copies, waits for them, and re-layouts  17.1 us
    reshape x1, local copies, waits for them, and re-layouts, local(): x_t = x_t.reshape(rows, n_x, 2, a_share * C)  13.4 us
    concatenate x1, other arithmetic, local(): y = jnp.concatenate([factor_db, y_other], axis=0)  12.2 us
  transfers between devices with their start and end apart: 5, of which 2 were waited for; matrix products, arithmetic and copies ran while one was open for 33% of the time, Pallas kernels for 0%

commit v1 on v0

v1 whole, which is shorter than its diff:
```python
import functools

import jax
import jax.numpy as jnp
from jax import lax
from jax.experimental import pallas as pl
from jax.experimental.pallas import tpu as pltpu
from jax.sharding import PartitionSpec as P

A = 128
B = 128
C = 128
D = 128
NA = 8
DC = 8
CHUNKS = 4


def ladder_kernel(xo_ref, xn_ref, yo_ref, yn_ref, t_ref, o_ref, xt, y, s, acc):
    rows = xo_ref.shape[0]
    half = y.shape[0] // 2
    n_blocks = y.shape[1] // (DC * B)

    @pl.when(pl.program_id(0) == 0)
    def _():
        if half > rows:
            y[...] = jnp.zeros_like(y)
        y[0:rows, :] = yo_ref[...]
        y[half:half + rows, :] = yn_ref[...]

    if half > rows:
        xt[...] = jnp.zeros_like(xt)
    xt[:, 0:rows] = xo_ref[...].T
    xt[:, half:half + rows] = xn_ref[...].T
    acc[...] = jnp.zeros_like(acc)

    def build(j, slot):
        for dd in range(0, DC, 2):
            cols = pl.ds(pl.multiple_of((j * DC + dd) * B, 2 * B), 2 * B)
            v = jnp.dot(xt[...], y[:, cols], preferred_element_type=jnp.float32)
            v = v.astype(jnp.bfloat16)
            for a in range(NA):
                for e in range(2):
                    s[slot, (dd + e) * C:(dd + e + 1) * C, a * B:(a + 1) * B] = v[
                        a * C:(a + 1) * C, e * B:(e + 1) * B
                    ]

    def contract(j, slot):
        tc = pl.ds(pl.multiple_of(j * DC * C, DC * C), DC * C)
        acc[...] += jnp.dot(t_ref[:, tc], s[slot], preferred_element_type=jnp.float32)

    build(0, 0)

    @pl.loop(0, n_blocks // 2 - 1)
    def _(h):
        build(2 * h + 1, 1)
        contract(2 * h, 0)
        build(2 * h + 2, 0)
        contract(2 * h + 1, 1)

    build(n_blocks - 1, 1)
    contract(n_blocks - 2, 0)
    contract(n_blocks - 1, 1)
    o_ref[0] = acc[...].astype(jnp.bfloat16)


def partial_ladder(xo, xn, yo, yn, t, chunk, n_chunks, n_out):
    rows, x_cols = xo.shape
    y_cols = yo.shape[1]
    n_ij = t.shape[0]
    na = x_cols // C // n_out // n_chunks
    steps = na // NA
    half = -(-rows // 16) * 16
    whole = lambda i: (0, 0)
    one = pl.Buffered(1)

    def x_map(i):
        return (0, (i // steps) * (n_chunks * steps) + chunk * steps + i % steps)

    return pl.pallas_call(
        ladder_kernel,
        grid=(n_out * steps,),
        in_specs=[
            pl.BlockSpec((rows, NA * C), x_map),
            pl.BlockSpec((rows, NA * C), x_map),
            pl.BlockSpec((rows, y_cols), whole, pipeline_mode=one),
            pl.BlockSpec((rows, y_cols), whole, pipeline_mode=one),
            pl.BlockSpec(t.shape, whole, pipeline_mode=one),
        ],
        out_specs=pl.BlockSpec((1, n_ij, NA * B), lambda i: (i // steps, 0, i % steps)),
        out_shape=jax.ShapeDtypeStruct((n_out, n_ij, na * B), jnp.bfloat16),
        scratch_shapes=[
            pltpu.VMEM((NA * C, 2 * half), jnp.bfloat16),
            pltpu.VMEM((2 * half, y_cols), jnp.bfloat16),
            pltpu.VMEM((2, DC * C, NA * B), jnp.bfloat16),
            pltpu.VMEM((n_ij, NA * B), jnp.float32),
        ],
        compiler_params=pltpu.CompilerParams(vmem_limit_bytes=56 << 20),
        cost_estimate=pl.CostEstimate(
            flops=2 * n_out * na * C * y_cols * (2 * rows + n_ij),
            bytes_accessed=4 * rows * (n_out * na * C + y_cols),
            transcendentals=0,
        ),
    )(xo, xn, yo, yn, t)


def local(amplitudes, factor_ca, factor_db):
    n_aux = lax.axis_size("aux")
    aux = lax.axis_index("aux")
    core = lax.rem(aux, 2)
    rows = factor_ca.shape[0]
    n_pair_rows = amplitudes.shape[0]
    d_half = D // 2
    a_share = A // n_aux
    swap = [(i, i ^ 1) for i in range(n_aux)]

    t_own = lax.dynamic_slice_in_dim(
        amplitudes.reshape(n_pair_rows, C, D).transpose(0, 2, 1),
        core * d_half + (aux // 2) * (d_half // 2),
        d_half // 2,
        1,
    ).reshape(n_pair_rows, d_half // 2 * C)
    n_pair = lax.axis_size("pair")
    t_send = jnp.broadcast_to(t_own[None], (n_pair,) + t_own.shape)
    t_first = lax.all_to_all(t_send, "pair", split_axis=0, concat_axis=0, tiled=True)
    t = t_first.reshape(n_pair * n_pair_rows, d_half // 2 * C)
    t_new = lax.ppermute(t, "aux", [(i, i ^ 2) for i in range(n_aux)])
    low = aux // 2 == 0
    t = jnp.concatenate([jnp.where(low, t, t_new), jnp.where(low, t_new, t)], axis=1)

    cols = d_half * B
    y_own = lax.dynamic_slice_in_dim(factor_db, core * cols, cols, 1)
    y_new = lax.ppermute(
        lax.dynamic_slice_in_dim(factor_db, (1 - core) * cols, cols, 1), "aux", swap
    )
    x_own, t_first = lax.optimization_barrier(
        (factor_ca.reshape(rows, C, A).transpose(0, 2, 1), t_first)
    )
    x_own = x_own.reshape(rows, A * C)
    x_new = lax.ppermute(x_own, "aux", swap)

    outs = []
    for chunk in range(CHUNKS):
        part = partial_ladder(x_own, x_new, y_own, y_new, t, chunk, CHUNKS, n_aux)
        total = lax.dynamic_index_in_dim(part, aux, 0, keepdims=False).astype(jnp.float32)
        for k in range(1, n_aux):
            give = lax.dynamic_index_in_dim(part, aux ^ k, 0, keepdims=False)
            hop = [(i, i ^ k) for i in range(n_aux)]
            total = total + lax.ppermute(give, "aux", hop).astype(jnp.float32)
        outs.append(
            lax.all_to_all(
                total.astype(jnp.bfloat16).reshape(n_pair, n_pair_rows, -1),
                "pair",
                split_axis=0,
                concat_axis=0,
                tiled=True,
            ).astype(jnp.float32).sum(0).astype(jnp.bfloat16)
        )
    return jnp.concatenate(outs, axis=1)


def solution(mesh):
    return jax.shard_map(
        local,
        mesh=mesh,
        in_specs=(P("pair", None), P(("pair", "aux"), None), P(("pair", "aux"), None)),
        out_specs=P("pair", "aux"),
        check_vma=False,
    )
```

time: 498 us -> 356 us (0.71)
  local copies, waits for them, and re-layouts: 155 us -> 42.6 us
  waiting for transfers between devices: 89.2 us -> 47.5 us
  starting transfers between devices: 3.4 us -> 37.3 us
  between operations: 13.5 us -> 0.14 us
  other arithmetic: 19.8 us -> 9.81 us
    dynamic_slice x3 -> x1, local copies, waits for them, and re-layouts: 111 us -> 6.35 us  [local(): lax.dynamic_slice_in_dim(factor_db, (1 - core) * cols, cols, 1)]
    reduce_scatter x1 -> x0, waiting for transfers between devices: 65.7 us -> none  [local(): lax.psum_scatter(total.astype(jnp.bfloat16), 'pair', scatter_dimension=0,...]
    all_to_all x0 -> x5, starting transfers between devices: none -> 26.5 us  [the longest x4 19.2 us: local(): lax.all_to_all(total.astype(jnp.bfloat16).reshape(n_pair, n_pair_rows, -1...]
    ppermute x2 -> x3, waiting for transfers between devices: 0.01 us -> 23.6 us  [the longest x1 23.6 us: local(): t_new = lax.ppermute(t, 'aux', [(i, i ^ 2) for i in range(n_aux)])]
    all_to_all x0 -> x5, waiting for transfers between devices: none -> 19.5 us  [the longest x4 11.2 us: local(): lax.all_to_all(total.astype(jnp.bfloat16).reshape(n_pair, n_pair_rows, -1...]
    ppermute x1 -> x12, waiting for transfers between devices: 23.5 us -> 4.33 us  [local(): total = total + lax.ppermute(give, 'aux', hop).astype(jnp.float32)]
    reshape x4 -> x1, local copies, waits for them, and re-layouts: 26.9 us -> 9.84 us  [local(): factor_ca.reshape(rows, C, A).transpose(0, 2, 1)]
    concatenate x2, other arithmetic: 17.5 us -> 2.17 us  [the longest x1 1.5 us: local(): jnp.concatenate([jnp.where(low, t, t_new), jnp.where(low, t_new, t)], axi...]
  transfers between devices with their start and end apart: 5 -> 20, of which waited for: 2 -> 5; matrix products, arithmetic and copies ran while one was open for 33% -> 10% of each run, Pallas kernels for 0% -> 46%
where the time goes in v1:
time: 356 us; the launch traced here: 355 us
  Pallas kernels  218 us (61%)
  waiting for transfers between devices  47.5 us (13%)
  local copies, waits for them, and re-layouts  42.6 us (12%)
  starting transfers between devices  37.3 us (10%)
  other arithmetic  9.81 us (3%)
    pallas_call x4, Pallas kernels, partial_ladder(): pl.pallas_call(ladder_kernel, grid=(n_out * steps,), in_specs=[pl.BlockSp...  218 us
    ppermute x1, waiting for transfers between devices, local(): t_new = lax.ppermute(t, 'aux', [(i, i ^ 2) for i in range(n_aux)])  23.6 us
    unnamed x5, local copies, waits for them, and re-layouts  20.5 us
    all_to_all x4, starting transfers between devices, local(): lax.all_to_all(total.astype(jnp.bfloat16).reshape(n_pair, n_pair_rows, -1...  19.2 us
    all_to_all x4, waiting for transfers between devices, local(): lax.all_to_all(total.astype(jnp.bfloat16).reshape(n_pair, n_pair_rows, -1...  11.2 us
    reshape x1, local copies, waits for them, and re-layouts, local(): factor_ca.reshape(rows, C, A).transpose(0, 2, 1)  9.84 us
    ppermute x12, starting transfers between devices, local(): total = total + lax.ppermute(give, 'aux', hop).astype(jnp.float32)  8.85 us
    all_to_all x1, waiting for transfers between devices, local(): lax.all_to_all(t_send, 'pair', split_axis=0, concat_axis=0, tiled=True)  8.37 us
  transfers between devices with their start and end apart: 20, of which 5 were waited for; matrix products, arithmetic and copies ran while one was open for 10% of the time, Pallas kernels for 46%

profile of v1, /device:TPU:0, one launch (start us, length us, event | category | flops | bytes accessed | tf_op | source)
XLA Modules:
  0.0 355.1 jit_solution(8066424734679777243)
XLA Ops:
  2.7 7.3 %all-to-all-start = ((bf16[8,16,4096]{2,1,0:T(8,128)(2,1)}), bf16[8,16,4096]{2,1,0:T(8,128)(2,1)S(1)}, u32[]{:S(2)}, u32[]{:S(2)}) async-start(bf16[8,16,4096]{2,1,0:T(8,128)(2,1)} %broadcast_in_dim.8), calls=%async_computation | async-start | bytes 2097152 | tf_op jit(solution)/shard_map/all_to_all | solution.py:125
  10.0 7.6 %copy.8 = bf16[25,8,128,128]{3,2,1,0:T(8,128)(2,1)} copy(bf16[25,8,128,128]{3,1,2,0:T(8,128)(2,1)} %bitcast.59) | data formatting | bytes 13107200
  17.5 9.8 %copy.5 = bf16[200,128,128]{1,2,0:T(8,128)(2,1)} copy(bf16[200,128,128]{2,1,0:T(8,128)(2,1)} %bitcast.58) | data formatting | bytes 13107200 | tf_op jit(solution)/shard_map/reshape | solution.py:137
  27.4 8.4 %all-to-all-done = bf16[8,16,4096]{2,1,0:T(8,128)(2,1)S(1)} async-done(((bf16[8,16,4096]{2,1,0:T(8,128)(2,1)}), bf16[8,16,4096]{2,1,0:T(8,128)(2,1)S(1)}, u32[]{:S(2)}, u32[]{:S(2)}) %all-to-all-start) | async-done | bytes 1048608 | tf_op jit(solution)/shard_map/all_to_all | solution.py:125
  35.8 11.6 %copy.14 = bf16[25,8,128,128]{3,1,2,0:T(8,128)(2,1)} copy(bf16[25,8,128,128]{3,2,1,0:T(8,128)(2,1)} %bitcast.57) | data formatting | bytes 13107200
  47.3 6.4 %constant_dynamic-slice_fusion = (bf16[200,8192]{1,0:T(8,128)(2,1)}, bf16[200,8192]{1,0:T(8,128)(2,1)}) fusion(bf16[200,16384]{1,0:T(8,128)(2,1)} %param.5, s32[]{:T(128)S(6)} %select_n.55, s32[]{:T(128)S(6)} %select_n.54), kind=kLoop, calls=%fused_computation.34 | loop fusion | bytes 13107208 | tf_op jit(solution)/shard_map/dynamic_slice | solution.py:134
  55.7 23.6 %collective-permute-done.2 = bf16[128,4096]{1,0:T(8,128)(2,1)S(1)} collective-permute-done((bf16[128,4096]{1,0:T(8,128)(2,1)S(1)}, bf16[128,4096]{1,0:T(8,128)(2,1)S(1)}, u32[]{:S(2)}, u32[]{:S(2)}) %collective-permute-start.2) | collective-permute-done | bytes 1048608 | tf_op jit(solution)/shard_map/ppermute | solution.py:127
  81.0 54.6 %shard_map.40 = bf16[4,128,1024]{2,1,0:T(8,128)(2,1)} custom-call(bf16[200,16384]{1,0:T(8,128)(2,1)} %bitcast.55.xo_ref, bf16[200,16384]{1,0:T(8,128)(2,1)} %collective-permute-done.xn_ref, bf16[200,8192]{1,0:T(8,128)(2,1)} %get-tuple-element.8.yo_ref, bf16[200,8192]{1,0:T(8,128)(2,1)} %collective-permute-done.1.yn_ref, bf16[128,8192]{1,0:T(8,128)(2,1)} %pad_maximum_fusion.t_ref), custom_call_target="tpu_custom_call" | custom-call | flops 35433480192 | bytes 9830400 | tf_op jit(solution)/shard_map/pallas_call | solution.py:80
  136.8 1.6 collective-permute-start.14
  138.9 54.4 %shard_map.39 = bf16[4,128,1024]{2,1,0:T(8,128)(2,1)} custom-call(bf16[200,16384]{1,0:T(8,128)(2,1)} %bitcast.55.xo_ref, bf16[200,16384]{1,0:T(8,128)(2,1)} %collective-permute-done.xn_ref, bf16[200,8192]{1,0:T(8,128)(2,1)} %get-tuple-element.8.yo_ref, bf16[200,8192]{1,0:T(8,128)(2,1)} %collective-permute-done.1.yn_ref, bf16[128,8192]{1,0:T(8,128)(2,1)} %pad_maximum_fusion.t_ref), custom_call_target="tpu_custom_call" | custom-call | flops 35433480192 | bytes 9830400 | tf_op jit(solution)/shard_map/pallas_call | solution.py:80
  194.6 1.6 collective-permute-start.11
  196.7 1.8 fusion.2
  198.6 3.6 %all-to-all-start.4 = ((bf16[8,16,1024]{2,1,0:T(8,128)(2,1)}), bf16[8,16,1024]{2,1,0:T(8,128)(2,1)S(1)}, u32[]{:S(2)}, u32[]{:S(2)}) async-start(bf16[8,16,1024]{2,1,0:T(8,128)(2,1)} %bitcast.22), calls=%async_computation.4 | async-start | bytes 524288 | tf_op jit(solution)/shard_map/all_to_all | solution.py:151
  202.2 54.4 %shard_map.37 = bf16[4,128,1024]{2,1,0:T(8,128)(2,1)} custom-call(bf16[200,16384]{1,0:T(8,128)(2,1)} %bitcast.55.xo_ref, bf16[200,16384]{1,0:T(8,128)(2,1)} %collective-permute-done.xn_ref, bf16[200,8192]{1,0:T(8,128)(2,1)} %get-tuple-element.8.yo_ref, bf16[200,8192]{1,0:T(8,128)(2,1)} %collective-permute-done.1.yn_ref, bf16[128,8192]{1,0:T(8,128)(2,1)} %pad_maximum_fusion.t_ref), custom_call_target="tpu_custom_call" | custom-call | flops 35433480192 | bytes 9830400 | tf_op jit(solution)/shard_map/pallas_call | solution.py:80
  260.0 1.8 fusion.5
  261.8 6.0 %all-to-all-start.3 = ((bf16[8,16,1024]{2,1,0:T(8,128)(2,1)}), bf16[8,16,1024]{2,1,0:T(8,128)(2,1)S(1)}, u32[]{:S(2)}, u32[]{:S(2)}) async-start(bf16[8,16,1024]{2,1,0:T(8,128)(2,1)} %bitcast.17), calls=%async_computation.3 | async-start | bytes 524288 | tf_op jit(solution)/shard_map/all_to_all | solution.py:151
  267.8 54.4 %shard_map.38 = bf16[4,128,1024]{2,1,0:T(8,128)(2,1)} custom-call(bf16[200,16384]{1,0:T(8,128)(2,1)} %bitcast.55.xo_ref, bf16[200,16384]{1,0:T(8,128)(2,1)} %collective-permute-done.xn_ref, bf16[200,8192]{1,0:T(8,128)(2,1)} %get-tuple-element.8.yo_ref, bf16[200,8192]{1,0:T(8,128)(2,1)} %collective-permute-done.1.yn_ref, bf16[128,8192]{1,0:T(8,128)(2,1)} %pad_maximum_fusion.t_ref), custom_call_target="tpu_custom_call" | custom-call | flops 35433480192 | bytes 9830400 | tf_op jit(solution)/shard_map/pallas_call | solution.py:80
  325.6 1.8 fusion.11
  327.4 6.0 %all-to-all-start.1 = ((bf16[8,16,1024]{2,1,0:T(8,128)(2,1)}), bf16[8,16,1024]{2,1,0:T(8,128)(2,1)S(1)}, u32[]{:S(2)}, u32[]{:S(2)}) async-start(bf16[8,16,1024]{2,1,0:T(8,128)(2,1)} %bitcast.7), calls=%async_computation.1 | async-start | bytes 524288 | tf_op jit(solution)/shard_map/all_to_all | solution.py:151
  333.4 4.3 %collective-permute-done.7 = bf16[128,1024]{1,0:T(8,128)(2,1)S(1)} collective-permute-done((bf16[128,1024]{1,0:T(8,128)(2,1)S(1)}, bf16[128,1024]{1,0:T(8,128)(2,1)S(1)}, u32[]{:S(2)}, u32[]{:S(2)}) %collective-permute-start.7) | collective-permute-done | bytes 262176 | tf_op jit(solution)/shard_map/ppermute | solution.py:149
  337.7 1.8 fusion.8
  339.5 2.7 all-to-all-done.1
  342.3 3.6 %all-to-all-start.2 = ((bf16[8,16,1024]{2,1,0:T(8,128)(2,1)}), bf16[8,16,1024]{2,1,0:T(8,128)(2,1)S(1)}, u32[]{:S(2)}, u32[]{:S(2)}) async-start(bf16[8,16,1024]{2,1,0:T(8,128)(2,1)} %bitcast.12), calls=%async_computation.2 | async-start | bytes 524288 | tf_op jit(solution)/shard_map/all_to_all | solution.py:151
  346.0 8.4 %all-to-all-done.2 = bf16[8,16,1024]{2,1,0:T(8,128)(2,1)S(1)} async-done(((bf16[8,16,1024]{2,1,0:T(8,128)(2,1)}), bf16[8,16,1024]{2,1,0:T(8,128)(2,1)S(1)}, u32[]{:S(2)}, u32[]{:S(2)}) %all-to-all-start.2) | async-done | bytes 262176 | tf_op jit(solution)/shard_map/all_to_all | solution.py:151
  (44 shorter events, 17.5 us)
Async XLA Ops:
  2.7 33.0 %all-to-all-start = ((bf16[8,16,4096]{2,1,0:T(8,128)(2,1)}), bf16[8,16,4096]{2,1,0:T(8,128)(2,1)S(1)}, u32[]{:S(2)}, u32[]{:S(2)}) async-start(bf16[8,16,4096]{2,1,0:T(8,128)(2,1)} %broadcast_in_dim.8), calls=%async_computation | async-start | bytes 2097152 | tf_op jit(solution)/shard_map/all_to_all | solution.py:125
  47.3 33.7 %collective-permute-start = (bf16[200,16384]{1,0:T(8,128)(2,1)}, bf16[200,16384]{1,0:T(8,128)(2,1)}, u32[]{:S(2)}, u32[]{:S(2)}) collective-permute-start(bf16[200,16384]{1,0:T(8,128)(2,1)} %bitcast.55.xo_ref), channel_id=1, source_target_pairs={{0,1},{1,0},{2,3},{3,2},{4,5},{5,4},{6,7},{7,6},{8,9},{9,8},{10,11... | collective-permute-start | bytes 19660808 | tf_op jit(solution)/shard_map/ppermute | solution.py:140
  53.7 27.3 %collective-permute-start.1 = (bf16[200,8192]{1,0:T(8,128)(2,1)}, bf16[200,8192]{1,0:T(8,128)(2,1)}, u32[]{:S(2)}, u32[]{:S(2)}) collective-permute-start(bf16[200,8192]{1,0:T(8,128)(2,1)} %get-tuple-element.7), channel_id=1, source_target_pairs={{0,1},{1,0},{2,3},{3,2},{4,5},{5,4},{6,7},{7,6},{8,9},{9,8},{10,11... | collective-permute-start | bytes 9830408 | tf_op jit(solution)/shard_map/ppermute | solution.py:133
  54.2 25.1 %collective-permute-start.2 = (bf16[128,4096]{1,0:T(8,128)(2,1)S(1)}, bf16[128,4096]{1,0:T(8,128)(2,1)S(1)}, u32[]{:S(2)}, u32[]{:S(2)}) collective-permute-start(bf16[128,4096]{1,0:T(8,128)(2,1)S(1)} %bitcast.60), channel_id=1, source_target_pairs={{0,2},{1,3},{2,0},{3,1},{4,6},{5,7},{6,4},{7,5},{8,10},{9,11},{10,... | collective-permute-start | bytes 3145736 | tf_op jit(solution)/shard_map/ppermute | solution.py:127
  136.7 59.5 %collective-permute-start.12 = (bf16[128,1024]{1,0:T(8,128)(2,1)S(1)}, bf16[128,1024]{1,0:T(8,128)(2,1)S(1)}, u32[]{:S(2)}, u32[]{:S(2)}) collective-permute-start(bf16[128,1024]{1,0:T(8,128)(2,1)S(1)} %get-tuple-element.20), channel_id=1, source_target_pairs={{0,1},{1,0},{2,3},{3,2},{4,5},{5,4},{6,7},{7,6},{8,9},{9,8},{10,11... | collective-permute-start | bytes 786440 | tf_op jit(solution)/shard_map/ppermute | solution.py:149
  136.8 59.9 %collective-permute-start.14 = (bf16[128,1024]{1,0:T(8,128)(2,1)S(1)}, bf16[128,1024]{1,0:T(8,128)(2,1)S(1)}, u32[]{:S(2)}, u32[]{:S(2)}) collective-permute-start(bf16[128,1024]{1,0:T(8,128)(2,1)S(1)} %get-tuple-element.21), channel_id=1, source_target_pairs={{0,3},{1,2},{2,1},{3,0},{4,7},{5,6},{6,5},{7,4},{8,11},{9,10},{10,... | collective-permute-start | bytes 786440 | tf_op jit(solution)/shard_map/ppermute | solution.py:149
  138.4 58.3 %collective-permute-start.13 = (bf16[128,1024]{1,0:T(8,128)(2,1)S(1)}, bf16[128,1024]{1,0:T(8,128)(2,1)S(1)}, u32[]{:S(2)}, u32[]{:S(2)}) collective-permute-start(bf16[128,1024]{1,0:T(8,128)(2,1)S(1)} %get-tuple-element.22), channel_id=1, source_target_pairs={{0,2},{1,3},{2,0},{3,1},{4,6},{5,7},{6,4},{7,5},{8,10},{9,11},{10,... | collective-permute-start | bytes 786440 | tf_op jit(solution)/shard_map/ppermute | solution.py:149
  194.5 65.0 %collective-permute-start.9 = (bf16[128,1024]{1,0:T(8,128)(2,1)S(1)}, bf16[128,1024]{1,0:T(8,128)(2,1)S(1)}, u32[]{:S(2)}, u32[]{:S(2)}) collective-permute-start(bf16[128,1024]{1,0:T(8,128)(2,1)S(1)} %get-tuple-element.17), channel_id=1, source_target_pairs={{0,1},{1,0},{2,3},{3,2},{4,5},{5,4},{6,7},{7,6},{8,9},{9,8},{10,11... | collective-permute-start | bytes 786440 | tf_op jit(solution)/shard_map/ppermute | solution.py:149
  194.6 65.4 %collective-permute-start.11 = (bf16[128,1024]{1,0:T(8,128)(2,1)S(1)}, bf16[128,1024]{1,0:T(8,128)(2,1)S(1)}, u32[]{:S(2)}, u32[]{:S(2)}) collective-permute-start(bf16[128,1024]{1,0:T(8,128)(2,1)S(1)} %get-tuple-element.18), channel_id=1, source_target_pairs={{0,3},{1,2},{2,1},{3,0},{4,7},{5,6},{6,5},{7,4},{8,11},{9,10},{10,... | collective-permute-start | bytes 786440 | tf_op jit(solution)/shard_map/ppermute | solution.py:149
  196.2 63.8 %collective-permute-start.10 = (bf16[128,1024]{1,0:T(8,128)(2,1)S(1)}, bf16[128,1024]{1,0:T(8,128)(2,1)S(1)}, u32[]{:S(2)}, u32[]{:S(2)}) collective-permute-start(bf16[128,1024]{1,0:T(8,128)(2,1)S(1)} %get-tuple-element.19), channel_id=1, source_target_pairs={{0,2},{1,3},{2,0},{3,1},{4,6},{5,7},{6,4},{7,5},{8,10},{9,11},{10,... | collective-permute-start | bytes 786440 | tf_op jit(solution)/shard_map/ppermute | solution.py:149
  198.6 63.3 %all-to-all-start.4 = ((bf16[8,16,1024]{2,1,0:T(8,128)(2,1)}), bf16[8,16,1024]{2,1,0:T(8,128)(2,1)S(1)}, u32[]{:S(2)}, u32[]{:S(2)}) async-start(bf16[8,16,1024]{2,1,0:T(8,128)(2,1)} %bitcast.22), calls=%async_computation.4 | async-start | bytes 524288 | tf_op jit(solution)/shard_map/all_to_all | solution.py:151
  257.8 67.3 %collective-permute-start.3 = (bf16[128,1024]{1,0:T(8,128)(2,1)S(1)}, bf16[128,1024]{1,0:T(8,128)(2,1)S(1)}, u32[]{:S(2)}, u32[]{:S(2)}) collective-permute-start(bf16[128,1024]{1,0:T(8,128)(2,1)S(1)} %get-tuple-element.11), channel_id=1, source_target_pairs={{0,1},{1,0},{2,3},{3,2},{4,5},{5,4},{6,7},{7,6},{8,9},{9,8},{10,11... | collective-permute-start | bytes 786440 | tf_op jit(solution)/shard_map/ppermute | solution.py:149
  257.9 67.7 %collective-permute-start.5 = (bf16[128,1024]{1,0:T(8,128)(2,1)S(1)}, bf16[128,1024]{1,0:T(8,128)(2,1)S(1)}, u32[]{:S(2)}, u32[]{:S(2)}) collective-permute-start(bf16[128,1024]{1,0:T(8,128)(2,1)S(1)} %get-tuple-element.12), channel_id=1, source_target_pairs={{0,3},{1,2},{2,1},{3,0},{4,7},{5,6},{6,5},{7,4},{8,11},{9,10},{10,... | collective-permute-start | bytes 786440 | tf_op jit(solution)/shard_map/ppermute | solution.py:149
  259.5 66.1 %collective-permute-start.4 = (bf16[128,1024]{1,0:T(8,128)(2,1)S(1)}, bf16[128,1024]{1,0:T(8,128)(2,1)S(1)}, u32[]{:S(2)}, u32[]{:S(2)}) collective-permute-start(bf16[128,1024]{1,0:T(8,128)(2,1)S(1)} %get-tuple-element.13), channel_id=1, source_target_pairs={{0,2},{1,3},{2,0},{3,1},{4,6},{5,7},{6,4},{7,5},{8,10},{9,11},{10,... | collective-permute-start | bytes 786440 | tf_op jit(solution)/shard_map/ppermute | solution.py:149
  261.8 65.6 %all-to-all-start.3 = ((bf16[8,16,1024]{2,1,0:T(8,128)(2,1)}), bf16[8,16,1024]{2,1,0:T(8,128)(2,1)S(1)}, u32[]{:S(2)}, u32[]{:S(2)}) async-start(bf16[8,16,1024]{2,1,0:T(8,128)(2,1)} %bitcast.17), calls=%async_computation.3 | async-start | bytes 524288 | tf_op jit(solution)/shard_map/all_to_all | solution.py:151
  323.4 10.1 %collective-permute-start.6 = (bf16[128,1024]{1,0:T(8,128)(2,1)S(1)}, bf16[128,1024]{1,0:T(8,128)(2,1)S(1)}, u32[]{:S(2)}, u32[]{:S(2)}) collective-permute-start(bf16[128,1024]{1,0:T(8,128)(2,1)S(1)} %get-tuple-element.14), channel_id=1, source_target_pairs={{0,1},{1,0},{2,3},{3,2},{4,5},{5,4},{6,7},{7,6},{8,9},{9,8},{10,11... | collective-permute-start | bytes 786440 | tf_op jit(solution)/shard_map/ppermute | solution.py:149
  323.4 10.0 %collective-permute-start.8 = (bf16[128,1024]{1,0:T(8,128)(2,1)S(1)}, bf16[128,1024]{1,0:T(8,128)(2,1)S(1)}, u32[]{:S(2)}, u32[]{:S(2)}) collective-permute-start(bf16[128,1024]{1,0:T(8,128)(2,1)S(1)} %get-tuple-element.15), channel_id=1, source_target_pairs={{0,3},{1,2},{2,1},{3,0},{4,7},{5,6},{6,5},{7,4},{8,11},{9,10},{10,... | collective-permute-start | bytes 786440 | tf_op jit(solution)/shard_map/ppermute | solution.py:149
  325.1 12.7 %collective-permute-start.7 = (bf16[128,1024]{1,0:T(8,128)(2,1)S(1)}, bf16[128,1024]{1,0:T(8,128)(2,1)S(1)}, u32[]{:S(2)}, u32[]{:S(2)}) collective-permute-start(bf16[128,1024]{1,0:T(8,128)(2,1)S(1)} %get-tuple-element.16), channel_id=1, source_target_pairs={{0,2},{1,3},{2,0},{3,1},{4,6},{5,7},{6,4},{7,5},{8,10},{9,11},{10,... | collective-permute-start | bytes 786440 | tf_op jit(solution)/shard_map/ppermute | solution.py:149
  327.4 14.9 %all-to-all-start.1 = ((bf16[8,16,1024]{2,1,0:T(8,128)(2,1)}), bf16[8,16,1024]{2,1,0:T(8,128)(2,1)S(1)}, u32[]{:S(2)}, u32[]{:S(2)}) async-start(bf16[8,16,1024]{2,1,0:T(8,128)(2,1)} %bitcast.7), calls=%async_computation.1 | async-start | bytes 524288 | tf_op jit(solution)/shard_map/all_to_all | solution.py:151
  342.3 12.2 %all-to-all-start.2 = ((bf16[8,16,1024]{2,1,0:T(8,128)(2,1)}), bf16[8,16,1024]{2,1,0:T(8,128)(2,1)S(1)}, u32[]{:S(2)}, u32[]{:S(2)}) async-start(bf16[8,16,1024]{2,1,0:T(8,128)(2,1)} %bitcast.12), calls=%async_computation.2 | async-start | bytes 524288 | tf_op jit(solution)/shard_map/all_to_all | solution.py:151
